TPU v7x, 128 devices: a whole 4x4x4 slice. The times are simulated.
128 devices in a mesh: db: 32 (over z, y, core), sub: 4 (over x).
Axes of the slice: x: 4, y: 4, z: 4, core: 2. Of those that a mesh axis runs over, the one named last changes fastest.
Arguments:
- codes: int32 [32768, 64], P('db', 'sub'), may hold values from 0 to 255
- tables: bfloat16 [2048, 64, 256], P('db', 'sub'), may hold values from 0.125 to 128, as said below
- limits: int32 [2048], replicated, may hold values from 3008 to 3263
Outputs:
- hit_ids: int32 [2048, 128], P(('db', 'sub'))
- hit_count: int32 [2048], P(('db', 'sub'))
Inputs may be any that keep to these rules, and one draw needn't show every extreme that they name: `tables`: each value is a bfloat16 number of at least 1/8 and at most 128.
All inputs are finite; a program needn't handle non-finite values.
Results may differ from a plain program's by a relative error of at most 0.000001.
Values may be sent and summed in bfloat16 or wider, within the bound.
No kernel may reach another device: no remote copies, remote signals or barrier semaphores. Data moves between devices by JAX's collectives and lax.ppermute only.
A program may use at most 128 MiB of HBM per device.

v0:
```python
import functools

import jax
import jax.numpy as jnp
from jax import lax
from jax.experimental import pallas as pl
from jax.experimental.pallas import tpu as pltpu
from jax.sharding import PartitionSpec as P

F8 = jnp.float8_e4m3fn
RANGES = 32
PARTS = 4
ROWS = 1024
QN = 64
QB = 16
K = 256
SLICE = ROWS // PARTS
CHUNK = 2048
GROUP = 4
LANES = 128
LOW_HALVES = {16: 0x0000FFFF, 8: 0x00FF00FF, 4: 0x0F0F0F0F, 2: 0x33333333, 1: 0x55555555}


def srl(word, by):
    return lax.shift_right_logical(word, jnp.full_like(word, by))


def popcount(word):
    word = word - (srl(word, 1) & 0x55555555)
    word = (word & 0x33333333) + (srl(word, 2) & 0x33333333)
    word = (word + srl(word, 4)) & 0x0F0F0F0F
    word = word + srl(word, 8)
    word = word + srl(word, 16)
    return word & 63


def lane_iota(rows):
    return lax.broadcasted_iota(jnp.int32, (rows, LANES), 1)


def picked(table, index):
    return jnp.take_along_axis(table, index, axis=1, mode="promise_in_bounds")


def exact_dot(a, b):
    return jnp.dot(
        a.astype(jnp.float32).astype(jnp.bfloat16),
        b.astype(jnp.float32).astype(jnp.bfloat16),
        preferred_element_type=jnp.float32,
    )


def pack_kernel(codes_ref, out_ref):
    codes = codes_ref[...]
    words = [
        codes[4 * word : 4 * word + 1]
        | (codes[4 * word + 1 : 4 * word + 2] << 8)
        | (codes[4 * word + 2 : 4 * word + 3] << 16)
        | (codes[4 * word + 3 : 4 * word + 4] << 24)
        for word in range(4)
    ]
    pieces = []
    for part in range(PARTS):
        for word in range(4):
            for side in range(2):
                at = part * SLICE + side * LANES
                pieces.append(words[word][:, at : at + LANES])
    packed = jnp.concatenate(pieces, axis=0)
    for copy in range(RANGES):
        out_ref[copy] = packed


def split_tables(tab_refs, wide_ref, hl_ref):
    wide = jnp.concatenate([ref[...].astype(jnp.float32).reshape(-1, K) for ref in tab_refs], axis=0)
    for side in range(2):
        wide_ref[side] = wide[:, side * LANES : (side + 1) * LANES]
    for m in range(16):
        for side in range(2):
            value = wide_ref[side, pl.ds(m, QN, stride=16), :]
            hi = value.astype(F8)
            lo = ((value - hi.astype(jnp.float32)) * 8.0).astype(F8)
            at = m * K + side * LANES
            hl_ref[0:QN, at : at + LANES] = hi
            hl_ref[QN : 2 * QN, at : at + LANES] = lo


def split_kernel(own_ref, before_ref, after_ref, hl0, hl1, hl3, wide_ref):
    split_tables((own_ref,), wide_ref, hl0)
    split_tables((before_ref,), wide_ref, hl1)
    split_tables((after_ref,), wide_ref, hl3)


def one_hot_group(words_ref, onehot_ref, chunk, quarter, first_word):
    centroid = lax.broadcasted_iota(jnp.int32, (K, LANES), 0).astype(jnp.int8)
    for block in range(CHUNK // LANES):
        source = (chunk * (CHUNK // SLICE) + block // 2) * PARTS + quarter
        for word in range(GROUP // 4):
            row = words_ref[source, pl.ds((first_word + word) * 2 + block % 2, 1), :]
            row = jnp.broadcast_to(row, (32, LANES))
            for byte in range(4):
                code = ((row >> (8 * byte)) & 255).astype(jnp.int8)
                code = jnp.concatenate([code] * (K // 32), axis=0)
                at = (word * 4 + byte) * K
                onehot_ref[at : at + K, block * LANES : (block + 1) * LANES] = jnp.where(
                    code == centroid, F8(1), F8(0)
                )


def hit_words(word, half):
    lane = lane_iota(QN)
    for step, low in LOW_HALVES.items():
        high = low << step
        high = high - (1 << 32) if high >= (1 << 31) else high
        after = pltpu.roll(word, LANES - step, 1)
        before = pltpu.roll(word, step, 1)
        word = jnp.where(
            (lane & step) == 0,
            (word & low) | ((after & low) << step),
            (word & high) | srl(before & high, step),
        )
    count = popcount(word)
    source = lax.broadcasted_iota(jnp.int32, (LANES, LANES), 0)
    target = lax.broadcasted_iota(jnp.int32, (LANES, LANES), 1)
    order = 4 * (source % 32) + source // 32
    ends = exact_dot(count, (order <= target).astype(jnp.float32)).astype(jnp.int32)
    in_range = half * 16 + order // 8 == target % RANGES
    return word, ends, exact_dot(count, in_range.astype(jnp.float32))


def list_hits(halves, position):
    lane = lane_iota(QN)
    (first_word, first_ends, first_hits), (last_word, last_ends, last_hits) = halves
    first_total = jnp.broadcast_to(first_ends[:, LANES - 1 :], (QN, LANES))
    second = lane >= first_total
    wanted = jnp.where(second, lane - first_total, lane)
    found = jnp.zeros((QN, LANES), jnp.int32)
    base = jnp.zeros((QN, LANES), jnp.int32)
    for step in (64, 32, 16, 8, 4, 2, 1):
        index = found + (step - 1)
        count = jnp.where(second, picked(last_ends, index), picked(first_ends, index))
        passed = count <= wanted
        found = jnp.where(passed, found + step, found)
        base = jnp.where(passed, count, base)
    at = 32 * (found & 3) + (found >> 2)
    word = jnp.where(second, picked(last_word, at), picked(first_word, at))
    rank = wanted - base
    bit = jnp.zeros((QN, LANES), jnp.int32)
    for step in (16, 8, 4, 2, 1):
        count = popcount(word & ((1 << step) - 1))
        passed = count <= rank
        rank = jnp.where(passed, rank - count, rank)
        word = jnp.where(passed, srl(word, step), word)
        bit = jnp.where(passed, bit + step, bit)
    local = jnp.where(second, 4096, 0) + 32 * found + bit
    ids = (local >> 8) * ROWS + position * SLICE + (local & (SLICE - 1))
    return ids, (first_hits + last_hits).astype(jnp.int32)


def score_kernel(
    limits_ref,
    words_ref,
    hl0,
    hl1_hbm,
    hl3_hbm,
    far_low_hbm,
    far_high_hbm,
    out0,
    out1,
    out2,
    out3,
    far_low,
    far_high,
    wide_ref,
    hl1,
    hl3,
    hl2,
    onehot_ref,
    lists_ref,
    copied,
):
    moves = ((hl1_hbm, hl1), (hl3_hbm, hl3), (far_low_hbm, far_low), (far_high_hbm, far_high))
    copies = [
        pltpu.make_async_copy(source, target, copied.at[at])
        for at, (source, target) in enumerate(moves)
    ]
    for copy in copies:
        copy.start()
    db, sub = lax.axis_index("db"), lax.axis_index("sub")
    lane = lane_iota(QN)
    mine = 64 * (db % 2) + lax.broadcasted_iota(jnp.int32, (QN, LANES), 0)
    row = jnp.broadcast_to(limits_ref[pl.ds(db // 2, 1), :], (QN, LANES)).astype(jnp.float32)
    limit = jnp.sum(jnp.where(lane == mine, row, 0.0), axis=1, keepdims=True)
    limit = jnp.broadcast_to(limit, (QN, LANES))

    halves = []
    bits = jnp.zeros((QN, LANES), jnp.int32)
    for chunk in range(RANGES * SLICE // CHUNK):
        total = jnp.zeros((2 * QN, CHUNK), jnp.float32)
        for group in range(64 // GROUP):
            shift = (0, 1, 3, 2)[group // 4]
            hl_ref = (hl0, hl1, hl2, hl3)[shift]
            if chunk == 0 and group in (4, 8):
                copies[group // 4 - 1].wait()
            if chunk == 0 and group == 12:
                copies[2].wait()
                copies[3].wait()
                split_tables((far_low, far_high), wide_ref, hl2)
            quarter = (sub + PARTS - shift) % PARTS
            one_hot_group(words_ref, onehot_ref, chunk, quarter, (group % 4) * (GROUP // 4))
            at = (group % 4) * GROUP * K
            total = total + jnp.dot(
                hl_ref[:, at : at + GROUP * K],
                onehot_ref[...],
                preferred_element_type=jnp.float32,
            )
        distance = total[:QN] + total[QN:] * 0.125
        for block in range(CHUNK // LANES):
            matched = distance[:, block * LANES : (block + 1) * LANES] <= limit
            at = (chunk * (CHUNK // LANES) + block) % 32
            bits = bits | jnp.where(matched, (1 << at) if at < 31 else -(1 << 31), 0)
        if (chunk + 1) * CHUNK % 4096 == 0:
            halves.append(hit_words(bits, len(halves)))
            bits = jnp.zeros((QN, LANES), jnp.int32)
    ids, hits = list_hits(halves, sub)
    lists_ref[:, :LANES] = ids
    lists_ref[:, LANES:] = hits
    for shift, out_ref in enumerate((out0, out1, out2, out3)):
        owner = (sub + shift) % PARTS
        out_ref[...] = lists_ref[pl.ds(pl.multiple_of(owner * QB, QB), QB), :]


def merge_kernel(l0, l1, l2, l3, ids_ref, count_ref):
    lane = lane_iota(QB)
    slices = [(lax.axis_index("sub") + PARTS - shift) % PARTS for shift in range(PARTS)]
    refs = (l0, l1, l2, l3)
    counts = jnp.zeros((QB, LANES), jnp.int32)
    for x, ref in zip(slices, refs):
        counts = jnp.where(lane // RANGES == x, ref[:, LANES:], counts)
    source = lax.broadcasted_iota(jnp.int32, (LANES, LANES), 0)
    segment = lax.broadcasted_iota(jnp.int32, (LANES, LANES), 1)
    order = 4 * (source % RANGES) + source // RANGES
    ends = exact_dot(counts, (order <= segment).astype(jnp.float32)).astype(jnp.int32)
    ahead = (order % 4 == segment % 4) & (order < segment)
    skipped = exact_dot(counts, ahead.astype(jnp.float32)).astype(jnp.int32)
    totals = lax.dot_general(
        jnp.ones((8, LANES), jnp.bfloat16),
        counts.astype(jnp.float32).astype(jnp.bfloat16),
        (((1,), (1,)), ((), ())),
        preferred_element_type=jnp.float32,
    )
    found = jnp.zeros((QB, LANES), jnp.int32)
    base = jnp.zeros((QB, LANES), jnp.int32)
    for step in (64, 32, 16, 8, 4, 2, 1):
        count = picked(ends, found + (step - 1))
        passed = count <= lane
        found = jnp.where(passed, found + step, found)
        base = jnp.where(passed, count, base)
    valid = lane < jnp.broadcast_to(ends[:, LANES - 1 :], (QB, LANES))
    index = jnp.where(valid, lane - base + picked(skipped, found), 0)
    value = jnp.zeros((QB, LANES), jnp.int32)
    for x, ref in zip(slices, refs):
        value = jnp.where(found % 4 == x, picked(ref[:, :LANES], index), value)
    ids_ref[...] = jnp.where(valid, value, -1)
    count_ref[...] = totals[:1].astype(jnp.int32)


VMEM = pl.BlockSpec(memory_space=pltpu.VMEM)
ANY = pl.BlockSpec(memory_space=pl.ANY)
PARAMS = pltpu.CompilerParams(vmem_limit_bytes=20 * 2**20)


def pack(codes):
    return pl.pallas_call(
        pack_kernel,
        out_shape=jax.ShapeDtypeStruct((RANGES, PARTS * 8, LANES), jnp.int32),
        in_specs=[VMEM],
        out_specs=VMEM,
        compiler_params=PARAMS,
        name="pack",
    )(codes.T)


def split(own, before, after):
    return pl.pallas_call(
        split_kernel,
        out_shape=[jax.ShapeDtypeStruct((2 * QN, 16 * K), F8)] * 3,
        in_specs=[VMEM] * 3,
        out_specs=[VMEM] * 3,
        scratch_shapes=[pltpu.VMEM((2, QN * 16, LANES), jnp.float32)],
        compiler_params=PARAMS,
        name="split",
    )(own, before, after)


def score(limits, words, tabs):
    return pl.pallas_call(
        score_kernel,
        out_shape=[jax.ShapeDtypeStruct((QB, 2 * LANES), jnp.int32)] * PARTS,
        in_specs=[VMEM] * 3 + [ANY] * 4,
        out_specs=[VMEM] * PARTS,
        scratch_shapes=[
            pltpu.VMEM((QN // 2, 16, K), jnp.bfloat16),
            pltpu.VMEM((QN // 2, 16, K), jnp.bfloat16),
            pltpu.VMEM((2, QN * 16, LANES), jnp.float32),
            pltpu.VMEM((2 * QN, 16 * K), F8),
            pltpu.VMEM((2 * QN, 16 * K), F8),
            pltpu.VMEM((2 * QN, 16 * K), F8),
            pltpu.VMEM((GROUP * K, CHUNK), F8),
            pltpu.VMEM((QN, 2 * LANES), jnp.int32),
            pltpu.SemaphoreType.DMA((4,)),
        ],
        compiler_params=PARAMS,
        name="score",
    )(limits, words, *tabs)


def merge(lists):
    return pl.pallas_call(
        merge_kernel,
        out_shape=(
            jax.ShapeDtypeStruct((QB, LANES), jnp.int32),
            jax.ShapeDtypeStruct((1, QB), jnp.int32),
        ),
        in_specs=[VMEM] * PARTS,
        out_specs=(VMEM, VMEM),
        compiler_params=PARAMS,
        name="merge",
    )(*lists)


def shifted(array, by):
    return lax.ppermute(array, "sub", [(x, (x + by) % PARTS) for x in range(PARTS)])


def per_device(codes, tables, limits):
    before, after = shifted(tables, 1), shifted(tables, -1)
    far_low = shifted(before[: QN // 2], 1)
    far_high = shifted(after[QN // 2 :], -1)
    sent = pack(codes).reshape(RANGES * PARTS, 8, LANES)
    words = lax.all_to_all(sent, ("db", "sub"), split_axis=0, concat_axis=0, tiled=True)
    lists = score(
        limits.reshape(16, LANES), words, (*split(tables, before, after), far_low, far_high)
    )
    received = [lists[0]] + [shifted(lists[k], k) for k in range(1, PARTS)]
    ids, count = merge(received)
    return ids, count.reshape(QB)


def solution(mesh):
    placed = (P("db", "sub"), P("db", "sub", None), P())
    return jax.shard_map(
        per_device,
        mesh=mesh,
        in_specs=placed,
        out_specs=(P(("db", "sub"), None), P(("db", "sub"))),
        check_vma=False,
    )
```

profile of v0, /device:TPU:0, one launch (start us, length us, event | category | flops | bytes accessed | tf_op | source)
XLA Modules:
  0.0 57.6 jit_solution(17683654028778262716)
XLA Ops:
  0.6 1.6 %collective-permute-start = (bf16[64,16,256]{2,1,0:T(8,128)(2,1)}, bf16[64,16,256]{2,1,0:T(8,128)(2,1)S(1)}, u32[]{:S(2)}, u32[]{:S(2)}) collective-permute-start(bf16[64,16,256]{2,1,0:T(8,128)(2,1)} %own_ref.1), channel_id=1, source_target_pairs={{0,1},{1,2},{2,3},{3,0},{4,5},{5,6},{6,7},{7,4},{8,9},{9,10},{10,1... | collective-permute-start | bytes 1572872 | tf_op jit(solution)/shard_map/ppermute | solution.py:332
  2.3 1.7 %collective-permute-start.1 = (bf16[64,16,256]{2,1,0:T(8,128)(2,1)}, bf16[64,16,256]{2,1,0:T(8,128)(2,1)S(1)}, u32[]{:S(2)}, u32[]{:S(2)}) collective-permute-start(bf16[64,16,256]{2,1,0:T(8,128)(2,1)} %own_ref.1), channel_id=1, source_target_pairs={{0,3},{1,0},{2,1},{3,2},{4,7},{5,4},{6,5},{7,6},{8,11},{9,8},{10,9... | collective-permute-start | bytes 1572872 | tf_op jit(solution)/shard_map/ppermute | solution.py:332
  3.9 0.0 copy-start.1
  3.9 0.8 %copy-done.1 = s32[1024,16]{0,1:T(8,128)S(1)} copy-done((s32[1024,16]{0,1:T(8,128)S(1)}, s32[1024,16]{0,1:T(8,128)}, u32[]{:S(2)}) %copy-start.1) | copy-done | bytes 65560
  4.8 0.9 %pack.1 = s32[32,32,128]{2,1,0:T(8,128)} custom-call(s32[16,1024]{1,0:T(8,128)S(1)} %bitcast.4), custom_call_target="tpu_custom_call" | custom-call | tf_op jit(solution)/shard_map/pack/pallas_call | solution.py:273
  5.6 9.9 %all-to-all-start = ((s32[128,8,128]{2,1,0:T(8,128)}), s32[128,8,128]{2,1,0:T(8,128)S(1)}, u32[]{:S(2)}, u32[]{:S(2)}) async-start(s32[128,8,128]{2,1,0:T(8,128)} %bitcast.2), calls=%async_computation | async-start | bytes 1048576 | tf_op jit(solution)/shard_map/all_to_all | solution.py:340
  15.6 0.0 copy-start
  15.6 0.1 collective-permute-done.before_ref
  15.7 0.7 %slice.8 = bf16[32,16,256]{2,1,0:T(8,128)(2,1)} slice(bf16[64,16,256]{2,1,0:T(8,128)(2,1)S(1)} %collective-permute-done.before_ref), slice={[0:32], [0:16], [0:256]} | slice | bytes 524288 | tf_op jit(solution)/shard_map/slice | solution.py:337
  16.4 0.9 %collective-permute-start.2 = (bf16[32,16,256]{2,1,0:T(8,128)(2,1)}, bf16[32,16,256]{2,1,0:T(8,128)(2,1)S(1)}, u32[]{:S(2)}, u32[]{:S(2)}) collective-permute-start(bf16[32,16,256]{2,1,0:T(8,128)(2,1)} %slice.8), channel_id=1, source_target_pairs={{0,1},{1,2},{2,3},{3,0},{4,5},{5,6},{6,7},{7,4},{8,9},{9,10},{10,1... | collective-permute-start | bytes 786440 | tf_op jit(solution)/shard_map/ppermute | solution.py:332
  17.3 0.0 collective-permute-done.1.after_ref
  17.3 0.7 %slice.9 = bf16[32,16,256]{2,1,0:T(8,128)(2,1)} slice(bf16[64,16,256]{2,1,0:T(8,128)(2,1)S(1)} %collective-permute-done.1.after_ref), slice={[32:64], [0:16], [0:256]} | slice | bytes 524288 | tf_op jit(solution)/shard_map/slice | solution.py:338
  18.0 2.4 %collective-permute-start.3 = (bf16[32,16,256]{2,1,0:T(8,128)(2,1)}, bf16[32,16,256]{2,1,0:T(8,128)(2,1)}, u32[]{:S(2)}, u32[]{:S(2)}) collective-permute-start(bf16[32,16,256]{2,1,0:T(8,128)(2,1)} %slice.9), channel_id=1, source_target_pairs={{0,3},{1,0},{2,1},{3,2},{4,7},{5,4},{6,5},{7,6},{8,11},{9,8},{10,9... | collective-permute-start | bytes 786440 | tf_op jit(solution)/shard_map/ppermute | solution.py:332
  20.4 0.0 copy-done
  20.4 0.0 copy-start.2
  20.4 1.5 %split.1 = (f8e4m3fn[128,4096]{1,0:T(32,128)(4,1)S(1)}, f8e4m3fn[128,4096]{1,0:T(32,128)(4,1)S(1)}, f8e4m3fn[128,4096]{1,0:T(32,128)(4,1)S(1)}) custom-call(bf16[64,16,256]{2,1,0:T(8,128)(2,1)S(1)} %copy-done, bf16[64,16,256]{2,1,0:T(8,128)(2,1)S(1)} %collective-permute-done.before_ref, bf16[64,16,256]{2,1,0:T(8,128)(2,1)S(1)} %collective-permute-done.1.after_ref), custom_call_target="tpu_custom_call" | custom-call | tf_op jit(solution)/shard_map/split/pallas_call | solution.py:284
  21.9 7.0 %all-to-all-done.words_ref = s32[128,8,128]{2,1,0:T(8,128)S(1)} async-done(((s32[128,8,128]{2,1,0:T(8,128)}), s32[128,8,128]{2,1,0:T(8,128)S(1)}, u32[]{:S(2)}, u32[]{:S(2)}) %all-to-all-start) | async-done | bytes 524320 | tf_op jit(solution)/shard_map/all_to_all | solution.py:340
  28.9 0.4 collective-permute-done.2.far_low_hbm
  29.3 0.0 collective-permute-done.3.far_high_hbm
  29.3 0.0 copy-done.2
  29.3 20.1 %score.1 = (s32[16,256]{1,0:T(8,128)S(1)}, s32[16,256]{1,0:T(8,128)S(1)}, s32[16,256]{1,0:T(8,128)S(1)}, s32[16,256]{1,0:T(8,128)S(1)}) custom-call(s32[16,128]{1,0:T(8,128)S(1)} %bitcast.5, s32[128,8,128]{2,1,0:T(8,128)S(1)} %all-to-all-done.words_ref, f8e4m3fn[128,4096]{1,0:T(32,128)(4,1)S(1)} %get-tuple-element.11.hl0, ...), custom_call_target="tpu_custom_call" | custom-call | tf_op jit(solution)/shard_map/score/pallas_call | solution.py:296
  49.5 0.4 collective-permute-start.4
  49.9 2.6 %collective-permute-start.5 = (s32[16,256]{1,0:T(8,128)S(1)}, s32[16,256]{1,0:T(8,128)S(1)}, u32[]{:S(2)}, u32[]{:S(2)}) collective-permute-start(s32[16,256]{1,0:T(8,128)S(1)} %get-tuple-element.16), channel_id=1, source_target_pairs={{0,2},{1,3},{2,0},{3,1},{4,6},{5,7},{6,4},{7,5},{8,10},{9,11},{10,... | collective-permute-start | bytes 49160 | tf_op jit(solution)/shard_map/ppermute | solution.py:332
  52.4 1.3 %collective-permute-start.6 = (s32[16,256]{1,0:T(8,128)S(1)}, s32[16,256]{1,0:T(8,128)S(1)}, u32[]{:S(2)}, u32[]{:S(2)}) collective-permute-start(s32[16,256]{1,0:T(8,128)S(1)} %get-tuple-element.17), channel_id=1, source_target_pairs={{0,3},{1,0},{2,1},{3,2},{4,7},{5,4},{6,5},{7,6},{8,11},{9,8},{10,9... | collective-permute-start | bytes 49160 | tf_op jit(solution)/shard_map/ppermute | solution.py:332
  53.7 0.8 %collective-permute-done.4.l1 = s32[16,256]{1,0:T(8,128)S(1)} collective-permute-done((s32[16,256]{1,0:T(8,128)S(1)}, s32[16,256]{1,0:T(8,128)S(1)}, u32[]{:S(2)}, u32[]{:S(2)}) %collective-permute-start.4) | collective-permute-done | bytes 16416 | tf_op jit(solution)/shard_map/ppermute | solution.py:332
  54.5 0.6 %collective-permute-done.5.l2 = s32[16,256]{1,0:T(8,128)S(1)} collective-permute-done((s32[16,256]{1,0:T(8,128)S(1)}, s32[16,256]{1,0:T(8,128)S(1)}, u32[]{:S(2)}, u32[]{:S(2)}) %collective-permute-start.5) | collective-permute-done | bytes 16416 | tf_op jit(solution)/shard_map/ppermute | solution.py:332
  55.1 1.1 %collective-permute-done.6.l3 = s32[16,256]{1,0:T(8,128)S(1)} collective-permute-done((s32[16,256]{1,0:T(8,128)S(1)}, s32[16,256]{1,0:T(8,128)S(1)}, u32[]{:S(2)}, u32[]{:S(2)}) %collective-permute-start.6) | collective-permute-done | bytes 16416 | tf_op jit(solution)/shard_map/ppermute | solution.py:332
  56.2 1.4 %merge.1 = (s32[16,128]{1,0:T(8,128)}, s32[1,16]{1,0:T(1,128)}) custom-call(s32[16,256]{1,0:T(8,128)S(1)} %get-tuple-element.14.l0, s32[16,256]{1,0:T(8,128)S(1)} %collective-permute-done.4.l1, s32[16,256]{1,0:T(8,128)S(1)} %collective-permute-done.5.l2, s32[16,256]{1,0:T(8,128)S(1)} %collective-permute-done.6.l3), custom_call_target="tpu_custom_call" | custom-call | tf_op jit(solution)/shard_map/merge/pallas_call | solution.py:318
Async XLA Ops:
  0.6 15.0 %collective-permute-start = (bf16[64,16,256]{2,1,0:T(8,128)(2,1)}, bf16[64,16,256]{2,1,0:T(8,128)(2,1)S(1)}, u32[]{:S(2)}, u32[]{:S(2)}) collective-permute-start(bf16[64,16,256]{2,1,0:T(8,128)(2,1)} %own_ref.1), channel_id=1, source_target_pairs={{0,1},{1,2},{2,3},{3,0},{4,5},{5,6},{6,7},{7,4},{8,9},{9,10},{10,1... | collective-permute-start | bytes 1572872 | tf_op jit(solution)/shard_map/ppermute | solution.py:332
  2.3 15.0 %collective-permute-start.1 = (bf16[64,16,256]{2,1,0:T(8,128)(2,1)}, bf16[64,16,256]{2,1,0:T(8,128)(2,1)S(1)}, u32[]{:S(2)}, u32[]{:S(2)}) collective-permute-start(bf16[64,16,256]{2,1,0:T(8,128)(2,1)} %own_ref.1), channel_id=1, source_target_pairs={{0,3},{1,0},{2,1},{3,2},{4,7},{5,4},{6,5},{7,6},{8,11},{9,8},{10,9... | collective-permute-start | bytes 1572872 | tf_op jit(solution)/shard_map/ppermute | solution.py:332
  3.9 0.8 %copy-start.1 = (s32[1024,16]{0,1:T(8,128)S(1)}, s32[1024,16]{0,1:T(8,128)}, u32[]{:S(2)}) copy-start(s32[1024,16]{0,1:T(8,128)} %param.3) | copy-start | bytes 196612
  5.6 23.3 %all-to-all-start = ((s32[128,8,128]{2,1,0:T(8,128)}), s32[128,8,128]{2,1,0:T(8,128)S(1)}, u32[]{:S(2)}, u32[]{:S(2)}) async-start(s32[128,8,128]{2,1,0:T(8,128)} %bitcast.2), calls=%async_computation | async-start | bytes 1048576 | tf_op jit(solution)/shard_map/all_to_all | solution.py:340
  15.6 4.8 %copy-start = (bf16[64,16,256]{2,1,0:T(8,128)(2,1)S(1)}, bf16[64,16,256]{2,1,0:T(8,128)(2,1)}, u32[]{:S(2)}) copy-start(bf16[64,16,256]{2,1,0:T(8,128)(2,1)} %own_ref.1) | copy-start | bytes 1572868
  16.4 12.9 %collective-permute-start.2 = (bf16[32,16,256]{2,1,0:T(8,128)(2,1)}, bf16[32,16,256]{2,1,0:T(8,128)(2,1)S(1)}, u32[]{:S(2)}, u32[]{:S(2)}) collective-permute-start(bf16[32,16,256]{2,1,0:T(8,128)(2,1)} %slice.8), channel_id=1, source_target_pairs={{0,1},{1,2},{2,3},{3,0},{4,5},{5,6},{6,7},{7,4},{8,9},{9,10},{10,1... | collective-permute-start | bytes 786440 | tf_op jit(solution)/shard_map/ppermute | solution.py:332
  18.0 11.3 %collective-permute-start.3 = (bf16[32,16,256]{2,1,0:T(8,128)(2,1)}, bf16[32,16,256]{2,1,0:T(8,128)(2,1)}, u32[]{:S(2)}, u32[]{:S(2)}) collective-permute-start(bf16[32,16,256]{2,1,0:T(8,128)(2,1)} %slice.9), channel_id=1, source_target_pairs={{0,3},{1,0},{2,1},{3,2},{4,7},{5,4},{6,5},{7,6},{8,11},{9,8},{10,9... | collective-permute-start | bytes 786440 | tf_op jit(solution)/shard_map/ppermute | solution.py:332
  20.4 8.9 %copy-start.2 = (s32[2048]{0:T(1024)S(1)}, s32[2048]{0:T(1024)}, u32[]{:S(2)}) copy-start(s32[2048]{0:T(1024)} %param.5) | copy-start | bytes 24580
  49.5 5.1 %collective-permute-start.4 = (s32[16,256]{1,0:T(8,128)S(1)}, s32[16,256]{1,0:T(8,128)S(1)}, u32[]{:S(2)}, u32[]{:S(2)}) collective-permute-start(s32[16,256]{1,0:T(8,128)S(1)} %get-tuple-element.15), channel_id=1, source_target_pairs={{0,1},{1,2},{2,3},{3,0},{4,5},{5,6},{6,7},{7,4},{8,9},{9,10},{10,1... | collective-permute-start | bytes 49160 | tf_op jit(solution)/shard_map/ppermute | solution.py:332
  49.9 5.2 %collective-permute-start.5 = (s32[16,256]{1,0:T(8,128)S(1)}, s32[16,256]{1,0:T(8,128)S(1)}, u32[]{:S(2)}, u32[]{:S(2)}) collective-permute-start(s32[16,256]{1,0:T(8,128)S(1)} %get-tuple-element.16), channel_id=1, source_target_pairs={{0,2},{1,3},{2,0},{3,1},{4,6},{5,7},{6,4},{7,5},{8,10},{9,11},{10,... | collective-permute-start | bytes 49160 | tf_op jit(solution)/shard_map/ppermute | solution.py:332
  52.4 3.7 %collective-permute-start.6 = (s32[16,256]{1,0:T(8,128)S(1)}, s32[16,256]{1,0:T(8,128)S(1)}, u32[]{:S(2)}, u32[]{:S(2)}) collective-permute-start(s32[16,256]{1,0:T(8,128)S(1)} %get-tuple-element.17), channel_id=1, source_target_pairs={{0,3},{1,0},{2,1},{3,2},{4,7},{5,4},{6,5},{7,6},{8,11},{9,8},{10,9... | collective-permute-start | bytes 49160 | tf_op jit(solution)/shard_map/ppermute | solution.py:332
where the time goes:
time: 57.8 us; the launch traced here: 57.6 us
  Pallas kernels  23.9 us (41%)
  starting transfers between devices  20.7 us (36%)
  waiting for transfers between devices  10 us (17%)
  local copies, waits for them, and re-layouts  2.32 us (4%)
  between operations  0.67 us (1%)
    pallas_call x1, Pallas kernels, score(): pl.pallas_call(score_kernel, out_shape=[jax.ShapeDtypeStruct((QB, 2 * LAN...  20.1 us
    ppermute x7, starting transfers between devices, shifted(): lax.ppermute(array, 'sub', [(x, (x + by) % PARTS) for x in range(PARTS)])  10.8 us
    all_to_all x1, starting transfers between devices, per_device(): lax.all_to_all(sent, ('db', 'sub'), split_axis=0, concat_axis=0, tiled=True)  9.93 us
    all_to_all x1, waiting for transfers between devices, per_device(): lax.all_to_all(sent, ('db', 'sub'), split_axis=0, concat_axis=0, tiled=True)  7.02 us
    ppermute x7, waiting for transfers between devices, shifted(): lax.ppermute(array, 'sub', [(x, (x + by) % PARTS) for x in range(PARTS)])  2.98 us
    pallas_call x1, Pallas kernels, split(): pl.pallas_call(split_kernel, out_shape=[jax.ShapeDtypeStruct((2 * QN, 16...  1.48 us
    pallas_call x1, Pallas kernels, merge(): pl.pallas_call(merge_kernel, out_shape=(jax.ShapeDtypeStruct((QB, LANES),...  1.4 us
  transfers between devices with their start and end apart: 8, of which 6 were waited for; matrix products, arithmetic and copies ran while one was open for 3% of the time, Pallas kernels for 4%

commit v1 on v0

--- a/solution.py
+++ b/solution.py
@@ -250,11 +250,13 @@
     )
     found = jnp.zeros((QB, LANES), jnp.int32)
     base = jnp.zeros((QB, LANES), jnp.int32)
-    for step in (64, 32, 16, 8, 4, 2, 1):
-        count = picked(ends, found + (step - 1))
-        passed = count <= lane
-        found = jnp.where(passed, found + step, found)
-        base = jnp.where(passed, count, base)
+    for step, ways in ((16, 8), (4, 4), (1, 4)):
+        start = found
+        for way in range(1, ways):
+            count = picked(ends, start + (way * step - 1))
+            passed = count <= lane
+            found = jnp.where(passed, start + way * step, found)
+            base = jnp.where(passed, count, base)
     valid = lane < jnp.broadcast_to(ends[:, LANES - 1 :], (QB, LANES))
     index = jnp.where(valid, lane - base + picked(skipped, found), 0)
     value = jnp.zeros((QB, LANES), jnp.int32)

time: 57.8 us -> 57.5 us (level)
  no operation moved by 1% of the time
where the time goes in v1:
time: 57.5 us; the launch traced here: 57.3 us
  Pallas kernels  23.6 us (41%)
  starting transfers between devices  20.7 us (36%)
  waiting for transfers between devices  10 us (17%)
  local copies, waits for them, and re-layouts  2.32 us (4%)
  between operations  0.67 us (1%)
    pallas_call x1, Pallas kernels, score(): pl.pallas_call(score_kernel, out_shape=[jax.ShapeDtypeStruct((QB, 2 * LAN...  20.1 us
    ppermute x7, starting transfers between devices, shifted(): lax.ppermute(array, 'sub', [(x, (x + by) % PARTS) for x in range(PARTS)])  10.8 us
    all_to_all x1, starting transfers between devices, per_device(): lax.all_to_all(sent, ('db', 'sub'), split_axis=0, concat_axis=0, tiled=True)  9.93 us
    all_to_all x1, waiting for transfers between devices, per_device(): lax.all_to_all(sent, ('db', 'sub'), split_axis=0, concat_axis=0, tiled=True)  7.02 us
    ppermute x7, waiting for transfers between devices, shifted(): lax.ppermute(array, 'sub', [(x, (x + by) % PARTS) for x in range(PARTS)])  2.98 us
    pallas_call x1, Pallas kernels, split(): pl.pallas_call(split_kernel, out_shape=[jax.ShapeDtypeStruct((2 * QN, 16...  1.48 us
    pallas_call x1, Pallas kernels, merge(): pl.pallas_call(merge_kernel, out_shape=(jax.ShapeDtypeStruct((QB, LANES),...  1.15 us
  transfers between devices with their start and end apart: 8, of which 6 were waited for; matrix products, arithmetic and copies ran while one was open for 3% of the time, Pallas kernels for 4%

profile of v1, /device:TPU:0, one launch (start us, length us, event | category | flops | bytes accessed | tf_op | source)
XLA Modules:
  0.0 57.3 jit_solution(2877437607700865485)
XLA Ops:
  0.6 1.6 %collective-permute-start = (bf16[64,16,256]{2,1,0:T(8,128)(2,1)}, bf16[64,16,256]{2,1,0:T(8,128)(2,1)S(1)}, u32[]{:S(2)}, u32[]{:S(2)}) collective-permute-start(bf16[64,16,256]{2,1,0:T(8,128)(2,1)} %own_ref.1), channel_id=1, source_target_pairs={{0,1},{1,2},{2,3},{3,0},{4,5},{5,6},{6,7},{7,4},{8,9},{9,10},{10,1... | collective-permute-start | bytes 1572872 | tf_op jit(solution)/shard_map/ppermute | solution.py:334
  2.3 1.7 %collective-permute-start.1 = (bf16[64,16,256]{2,1,0:T(8,128)(2,1)}, bf16[64,16,256]{2,1,0:T(8,128)(2,1)S(1)}, u32[]{:S(2)}, u32[]{:S(2)}) collective-permute-start(bf16[64,16,256]{2,1,0:T(8,128)(2,1)} %own_ref.1), channel_id=1, source_target_pairs={{0,3},{1,0},{2,1},{3,2},{4,7},{5,4},{6,5},{7,6},{8,11},{9,8},{10,9... | collective-permute-start | bytes 1572872 | tf_op jit(solution)/shard_map/ppermute | solution.py:334
  3.9 0.0 copy-start.1
  3.9 0.8 %copy-done.1 = s32[1024,16]{0,1:T(8,128)S(1)} copy-done((s32[1024,16]{0,1:T(8,128)S(1)}, s32[1024,16]{0,1:T(8,128)}, u32[]{:S(2)}) %copy-start.1) | copy-done | bytes 65560
  4.8 0.9 %pack.1 = s32[32,32,128]{2,1,0:T(8,128)} custom-call(s32[16,1024]{1,0:T(8,128)S(1)} %bitcast.4), custom_call_target="tpu_custom_call" | custom-call | tf_op jit(solution)/shard_map/pack/pallas_call | solution.py:275
  5.6 9.9 %all-to-all-start = ((s32[128,8,128]{2,1,0:T(8,128)}), s32[128,8,128]{2,1,0:T(8,128)S(1)}, u32[]{:S(2)}, u32[]{:S(2)}) async-start(s32[128,8,128]{2,1,0:T(8,128)} %bitcast.2), calls=%async_computation | async-start | bytes 1048576 | tf_op jit(solution)/shard_map/all_to_all | solution.py:342
  15.6 0.0 copy-start
  15.6 0.1 collective-permute-done.before_ref
  15.7 0.7 %slice.8 = bf16[32,16,256]{2,1,0:T(8,128)(2,1)} slice(bf16[64,16,256]{2,1,0:T(8,128)(2,1)S(1)} %collective-permute-done.before_ref), slice={[0:32], [0:16], [0:256]} | slice | bytes 524288 | tf_op jit(solution)/shard_map/slice | solution.py:339
  16.4 0.9 %collective-permute-start.2 = (bf16[32,16,256]{2,1,0:T(8,128)(2,1)}, bf16[32,16,256]{2,1,0:T(8,128)(2,1)S(1)}, u32[]{:S(2)}, u32[]{:S(2)}) collective-permute-start(bf16[32,16,256]{2,1,0:T(8,128)(2,1)} %slice.8), channel_id=1, source_target_pairs={{0,1},{1,2},{2,3},{3,0},{4,5},{5,6},{6,7},{7,4},{8,9},{9,10},{10,1... | collective-permute-start | bytes 786440 | tf_op jit(solution)/shard_map/ppermute | solution.py:334
  17.3 0.0 collective-permute-done.1.after_ref
  17.3 0.7 %slice.9 = bf16[32,16,256]{2,1,0:T(8,128)(2,1)} slice(bf16[64,16,256]{2,1,0:T(8,128)(2,1)S(1)} %collective-permute-done.1.after_ref), slice={[32:64], [0:16], [0:256]} | slice | bytes 524288 | tf_op jit(solution)/shard_map/slice | solution.py:340
  18.0 2.4 %collective-permute-start.3 = (bf16[32,16,256]{2,1,0:T(8,128)(2,1)}, bf16[32,16,256]{2,1,0:T(8,128)(2,1)}, u32[]{:S(2)}, u32[]{:S(2)}) collective-permute-start(bf16[32,16,256]{2,1,0:T(8,128)(2,1)} %slice.9), channel_id=1, source_target_pairs={{0,3},{1,0},{2,1},{3,2},{4,7},{5,4},{6,5},{7,6},{8,11},{9,8},{10,9... | collective-permute-start | bytes 786440 | tf_op jit(solution)/shard_map/ppermute | solution.py:334
  20.4 0.0 copy-done
  20.4 0.0 copy-start.2
  20.4 1.5 %split.1 = (f8e4m3fn[128,4096]{1,0:T(32,128)(4,1)S(1)}, f8e4m3fn[128,4096]{1,0:T(32,128)(4,1)S(1)}, f8e4m3fn[128,4096]{1,0:T(32,128)(4,1)S(1)}) custom-call(bf16[64,16,256]{2,1,0:T(8,128)(2,1)S(1)} %copy-done, bf16[64,16,256]{2,1,0:T(8,128)(2,1)S(1)} %collective-permute-done.before_ref, bf16[64,16,256]{2,1,0:T(8,128)(2,1)S(1)} %collective-permute-done.1.after_ref), custom_call_target="tpu_custom_call" | custom-call | tf_op jit(solution)/shard_map/split/pallas_call | solution.py:286
  21.9 7.0 %all-to-all-done.words_ref = s32[128,8,128]{2,1,0:T(8,128)S(1)} async-done(((s32[128,8,128]{2,1,0:T(8,128)}), s32[128,8,128]{2,1,0:T(8,128)S(1)}, u32[]{:S(2)}, u32[]{:S(2)}) %all-to-all-start) | async-done | bytes 524320 | tf_op jit(solution)/shard_map/all_to_all | solution.py:342
  28.9 0.4 collective-permute-done.2.far_low_hbm
  29.3 0.0 collective-permute-done.3.far_high_hbm
  29.3 0.0 copy-done.2
  29.3 20.1 %score.1 = (s32[16,256]{1,0:T(8,128)S(1)}, s32[16,256]{1,0:T(8,128)S(1)}, s32[16,256]{1,0:T(8,128)S(1)}, s32[16,256]{1,0:T(8,128)S(1)}) custom-call(s32[16,128]{1,0:T(8,128)S(1)} %bitcast.5, s32[128,8,128]{2,1,0:T(8,128)S(1)} %all-to-all-done.words_ref, f8e4m3fn[128,4096]{1,0:T(32,128)(4,1)S(1)} %get-tuple-element.11.hl0, ...), custom_call_target="tpu_custom_call" | custom-call | tf_op jit(solution)/shard_map/score/pallas_call | solution.py:298
  49.5 0.4 collective-permute-start.4
  49.9 2.6 %collective-permute-start.5 = (s32[16,256]{1,0:T(8,128)S(1)}, s32[16,256]{1,0:T(8,128)S(1)}, u32[]{:S(2)}, u32[]{:S(2)}) collective-permute-start(s32[16,256]{1,0:T(8,128)S(1)} %get-tuple-element.16), channel_id=1, source_target_pairs={{0,2},{1,3},{2,0},{3,1},{4,6},{5,7},{6,4},{7,5},{8,10},{9,11},{10,... | collective-permute-start | bytes 49160 | tf_op jit(solution)/shard_map/ppermute | solution.py:334
  52.4 1.3 %collective-permute-start.6 = (s32[16,256]{1,0:T(8,128)S(1)}, s32[16,256]{1,0:T(8,128)S(1)}, u32[]{:S(2)}, u32[]{:S(2)}) collective-permute-start(s32[16,256]{1,0:T(8,128)S(1)} %get-tuple-element.17), channel_id=1, source_target_pairs={{0,3},{1,0},{2,1},{3,2},{4,7},{5,4},{6,5},{7,6},{8,11},{9,8},{10,9... | collective-permute-start | bytes 49160 | tf_op jit(solution)/shard_map/ppermute | solution.py:334
  53.7 0.8 %collective-permute-done.4.l1 = s32[16,256]{1,0:T(8,128)S(1)} collective-permute-done((s32[16,256]{1,0:T(8,128)S(1)}, s32[16,256]{1,0:T(8,128)S(1)}, u32[]{:S(2)}, u32[]{:S(2)}) %collective-permute-start.4) | collective-permute-done | bytes 16416 | tf_op jit(solution)/shard_map/ppermute | solution.py:334
  54.5 0.6 %collective-permute-done.5.l2 = s32[16,256]{1,0:T(8,128)S(1)} collective-permute-done((s32[16,256]{1,0:T(8,128)S(1)}, s32[16,256]{1,0:T(8,128)S(1)}, u32[]{:S(2)}, u32[]{:S(2)}) %collective-permute-start.5) | collective-permute-done | bytes 16416 | tf_op jit(solution)/shard_map/ppermute | solution.py:334
  55.1 1.1 %collective-permute-done.6.l3 = s32[16,256]{1,0:T(8,128)S(1)} collective-permute-done((s32[16,256]{1,0:T(8,128)S(1)}, s32[16,256]{1,0:T(8,128)S(1)}, u32[]{:S(2)}, u32[]{:S(2)}) %collective-permute-start.6) | collective-permute-done | bytes 16416 | tf_op jit(solution)/shard_map/ppermute | solution.py:334
  56.2 1.2 %merge.1 = (s32[16,128]{1,0:T(8,128)}, s32[1,16]{1,0:T(1,128)}) custom-call(s32[16,256]{1,0:T(8,128)S(1)} %get-tuple-element.14.l0, s32[16,256]{1,0:T(8,128)S(1)} %collective-permute-done.4.l1, s32[16,256]{1,0:T(8,128)S(1)} %collective-permute-done.5.l2, s32[16,256]{1,0:T(8,128)S(1)} %collective-permute-done.6.l3), custom_call_target="tpu_custom_call" | custom-call | tf_op jit(solution)/shard_map/merge/pallas_call | solution.py:320
Async XLA Ops:
  0.6 15.0 %collective-permute-start = (bf16[64,16,256]{2,1,0:T(8,128)(2,1)}, bf16[64,16,256]{2,1,0:T(8,128)(2,1)S(1)}, u32[]{:S(2)}, u32[]{:S(2)}) collective-permute-start(bf16[64,16,256]{2,1,0:T(8,128)(2,1)} %own_ref.1), channel_id=1, source_target_pairs={{0,1},{1,2},{2,3},{3,0},{4,5},{5,6},{6,7},{7,4},{8,9},{9,10},{10,1... | collective-permute-start | bytes 1572872 | tf_op jit(solution)/shard_map/ppermute | solution.py:334
  2.3 15.0 %collective-permute-start.1 = (bf16[64,16,256]{2,1,0:T(8,128)(2,1)}, bf16[64,16,256]{2,1,0:T(8,128)(2,1)S(1)}, u32[]{:S(2)}, u32[]{:S(2)}) collective-permute-start(bf16[64,16,256]{2,1,0:T(8,128)(2,1)} %own_ref.1), channel_id=1, source_target_pairs={{0,3},{1,0},{2,1},{3,2},{4,7},{5,4},{6,5},{7,6},{8,11},{9,8},{10,9... | collective-permute-start | bytes 1572872 | tf_op jit(solution)/shard_map/ppermute | solution.py:334
  3.9 0.8 %copy-start.1 = (s32[1024,16]{0,1:T(8,128)S(1)}, s32[1024,16]{0,1:T(8,128)}, u32[]{:S(2)}) copy-start(s32[1024,16]{0,1:T(8,128)} %param.3) | copy-start | bytes 196612
  5.6 23.3 %all-to-all-start = ((s32[128,8,128]{2,1,0:T(8,128)}), s32[128,8,128]{2,1,0:T(8,128)S(1)}, u32[]{:S(2)}, u32[]{:S(2)}) async-start(s32[128,8,128]{2,1,0:T(8,128)} %bitcast.2), calls=%async_computation | async-start | bytes 1048576 | tf_op jit(solution)/shard_map/all_to_all | solution.py:342
  15.6 4.8 %copy-start = (bf16[64,16,256]{2,1,0:T(8,128)(2,1)S(1)}, bf16[64,16,256]{2,1,0:T(8,128)(2,1)}, u32[]{:S(2)}) copy-start(bf16[64,16,256]{2,1,0:T(8,128)(2,1)} %own_ref.1) | copy-start | bytes 1572868
  16.4 12.9 %collective-permute-start.2 = (bf16[32,16,256]{2,1,0:T(8,128)(2,1)}, bf16[32,16,256]{2,1,0:T(8,128)(2,1)S(1)}, u32[]{:S(2)}, u32[]{:S(2)}) collective-permute-start(bf16[32,16,256]{2,1,0:T(8,128)(2,1)} %slice.8), channel_id=1, source_target_pairs={{0,1},{1,2},{2,3},{3,0},{4,5},{5,6},{6,7},{7,4},{8,9},{9,10},{10,1... | collective-permute-start | bytes 786440 | tf_op jit(solution)/shard_map/ppermute | solution.py:334
  18.0 11.3 %collective-permute-start.3 = (bf16[32,16,256]{2,1,0:T(8,128)(2,1)}, bf16[32,16,256]{2,1,0:T(8,128)(2,1)}, u32[]{:S(2)}, u32[]{:S(2)}) collective-permute-start(bf16[32,16,256]{2,1,0:T(8,128)(2,1)} %slice.9), channel_id=1, source_target_pairs={{0,3},{1,0},{2,1},{3,2},{4,7},{5,4},{6,5},{7,6},{8,11},{9,8},{10,9... | collective-permute-start | bytes 786440 | tf_op jit(solution)/shard_map/ppermute | solution.py:334
  20.4 8.9 %copy-start.2 = (s32[2048]{0:T(1024)S(1)}, s32[2048]{0:T(1024)}, u32[]{:S(2)}) copy-start(s32[2048]{0:T(1024)} %param.5) | copy-start | bytes 24580
  49.5 5.1 %collective-permute-start.4 = (s32[16,256]{1,0:T(8,128)S(1)}, s32[16,256]{1,0:T(8,128)S(1)}, u32[]{:S(2)}, u32[]{:S(2)}) collective-permute-start(s32[16,256]{1,0:T(8,128)S(1)} %get-tuple-element.15), channel_id=1, source_target_pairs={{0,1},{1,2},{2,3},{3,0},{4,5},{5,6},{6,7},{7,4},{8,9},{9,10},{10,1... | collective-permute-start | bytes 49160 | tf_op jit(solution)/shard_map/ppermute | solution.py:334
  49.9 5.2 %collective-permute-start.5 = (s32[16,256]{1,0:T(8,128)S(1)}, s32[16,256]{1,0:T(8,128)S(1)}, u32[]{:S(2)}, u32[]{:S(2)}) collective-permute-start(s32[16,256]{1,0:T(8,128)S(1)} %get-tuple-element.16), channel_id=1, source_target_pairs={{0,2},{1,3},{2,0},{3,1},{4,6},{5,7},{6,4},{7,5},{8,10},{9,11},{10,... | collective-permute-start | bytes 49160 | tf_op jit(solution)/shard_map/ppermute | solution.py:334
  52.4 3.7 %collective-permute-start.6 = (s32[16,256]{1,0:T(8,128)S(1)}, s32[16,256]{1,0:T(8,128)S(1)}, u32[]{:S(2)}, u32[]{:S(2)}) collective-permute-start(s32[16,256]{1,0:T(8,128)S(1)} %get-tuple-element.17), channel_id=1, source_target_pairs={{0,3},{1,0},{2,1},{3,2},{4,7},{5,4},{6,5},{7,6},{8,11},{9,8},{10,9... | collective-permute-start | bytes 49160 | tf_op jit(solution)/shard_map/ppermute | solution.py:334
